TPU v7x, 512 devices: a whole 4x8x8 slice. The times are simulated.
512 devices in a mesh: tm: 8 (over x, core), row: 64 (over y, z).
Axes of the slice: x: 4, y: 8, z: 8, core: 2. Of those that a mesh axis runs over, the one named last changes fastest.
Arguments:
- forcing: float32 [8, 2048, 2048], P('tm', 'row'), may hold values from -6 to 6
- rate_class: int32 [2048, 2048], P('row'), may hold values from 0 to 15
- rate_table: float32 [16], replicated, may hold values from 0.95 to 0.999
- row_class: int32 [2048], replicated, may hold values from 0 to 1
- col_class: int32 [2048], replicated, may hold values from 0 to 1
- inverse_offsets: float32 [2, 512, 512], P(None, 'row'), may hold values from -0.25 to 0.25
Outputs:
- covariance_field: float32 [8, 2048, 2048], P('tm', 'row')
- adjoint_field: float32 [8, 2048, 2048], P('tm', 'row')
All inputs are finite; a program needn't handle non-finite values.
Results may differ from a plain program's by a relative error of at most 0.0001.
Values sent between devices are 32-bit elements; how exact they have to be, the bound alone decides.
No kernel may reach another device: no remote copies, remote signals or barrier semaphores. Data moves between devices by JAX's collectives and lax.ppermute only.
A program may use at most 64 MiB of HBM per device.

v0:
```python
import jax
import jax.numpy as jnp
from jax import lax
from jax.sharding import PartitionSpec as P


def carried_in(part, axis, combine, identity, reverse):
    count = lax.axis_size(axis)
    place = lax.axis_index(axis)
    ahead = count - 1 - place if reverse else place
    gathered = jax.tree.map(lambda a: lax.all_gather(a, axis), part)
    state = jax.tree.map(lambda a, e: jnp.zeros_like(a) + jnp.asarray(e, a.dtype), part, identity)

    def one(turn, state):
        source = count - 1 - turn if reverse else turn
        return combine(
            state, jax.tree.map(lambda a: lax.dynamic_index_in_dim(a, source, 0, False), gathered)
        )

    return lax.fori_loop(0, ahead, one, state)


def lookup(labels, table):
    result = jnp.zeros(labels.shape, jnp.float32)
    for table_row in range(table.shape[0]):
        result = jnp.where(labels == table_row, table[table_row], result)
    return result


def rows_forward(forcing, offsets, my_rows):
    steps_here, row_count, grid_size = forcing.shape
    block_size = offsets.shape[1]
    pieces = forcing.reshape(steps_here, row_count, grid_size // block_size, block_size)

    def apply_class(category):
        return jnp.einsum(
            "trbi,ij->tbjr", pieces, offsets[category], precision=lax.Precision.HIGHEST
        )

    result = apply_class(0)
    category = 1
    result = jnp.where((my_rows == category).reshape(1, 1, 1, -1), apply_class(category), result)
    result = result + pieces.transpose(0, 2, 3, 1)
    return result.reshape(steps_here, grid_size, row_count)


def rows_adjoint(spread, offsets, my_rows):
    steps_here, grid_size, row_count = spread.shape
    block_size = offsets.shape[1]
    pieces = spread.reshape(steps_here, grid_size // block_size, block_size, row_count)

    def apply_class(category):
        return jnp.einsum(
            "tbjr,ij->trbi", pieces, offsets[category], precision=lax.Precision.HIGHEST
        )

    result = apply_class(0)
    category = 1
    result = jnp.where((my_rows == category).reshape(1, -1, 1, 1), apply_class(category), result)
    result = result + pieces.transpose(0, 3, 1, 2)
    return result.reshape(steps_here, row_count, grid_size)


def columns_apply(items, offsets, my_cols, adjoint):
    count_items, col_count, grid_size = items.shape
    block_size = offsets.shape[1]
    pieces = items.reshape(count_items, col_count, grid_size // block_size, block_size)
    pattern = "tcbj,ij->tcbi" if adjoint else "tcbi,ij->tcbj"

    def apply_class(category):
        return jnp.einsum(pattern, pieces, offsets[category], precision=lax.Precision.HIGHEST)

    result = apply_class(0)
    category = 1
    result = jnp.where((my_cols == category).reshape(1, -1, 1, 1), apply_class(category), result)
    result = result + pieces
    return result.reshape(count_items, col_count, grid_size)


def to_rows(column_field):
    return lax.all_to_all(column_field, "row", split_axis=2, concat_axis=1, tiled=True)


def affine_join(earlier, latter):
    return (earlier[0] * latter[0], latter[0] * earlier[1] + latter[1])


def forward_link(span, final_state):
    identity_pair = (jnp.ones_like(span), jnp.zeros_like(final_state))
    _, incoming = carried_in((span, final_state), "tm", affine_join, identity_pair, False)
    return incoming


def adjoint_link(span, first_state):
    identity_pair = (jnp.ones_like(span), jnp.zeros_like(first_state))
    _, incoming = carried_in((span, first_state), "tm", affine_join, identity_pair, True)
    return incoming


def chain_powers(decays):
    running = jnp.ones_like(decays)
    running = running * decays
    powers = [running]
    return powers


def forward_full(source, decays, scaled):
    carried = jnp.zeros_like(decays)
    carried = decays * carried + scaled * source[0]
    powers = chain_powers(decays)
    incoming = forward_link(powers[-1], carried)
    return jnp.stack([carried + powers[0] * incoming])


def adjoint_full(source, decays, scaled):
    length = source.shape[0]
    carried = jnp.zeros_like(decays)
    history = [None] * length
    carried = decays * carried + scaled * source[0]
    history[0] = carried
    powers = chain_powers(decays)
    incoming = adjoint_link(powers[-1], carried)
    return jnp.stack([history[0] + powers[length - 1] * incoming])


def per_device(forcing, rate_class, rate_table, row_class, col_class, inverse_offsets):
    row_count = forcing.shape[1]
    offsets = lax.all_gather(inverse_offsets, "row", axis=1, tiled=True)
    first_row = lax.axis_index("row") * row_count
    my_rows = lax.dynamic_slice_in_dim(row_class, first_row, row_count)
    my_cols = lax.dynamic_slice_in_dim(col_class, first_row, row_count)
    row_solved = rows_forward(forcing, offsets, my_rows)
    smoothed = columns_apply(
        lax.all_to_all(row_solved, "row", split_axis=1, concat_axis=2, tiled=True),
        offsets,
        my_cols,
        False,
    )
    decays = lookup(rate_class.T, rate_table)
    scaled = jnp.sqrt(1.0 - decays * decays)
    forward_rows = forward_full(to_rows(smoothed), decays, scaled)
    covariance_field = forward_rows.transpose(0, 2, 1)
    backward = adjoint_full(forward_rows, decays, scaled)
    spread = to_rows(
        columns_apply(
            lax.all_to_all(backward, "row", split_axis=1, concat_axis=2, tiled=True),
            offsets,
            my_cols,
            True,
        )
    )
    adjoint_field = rows_adjoint(spread, offsets, my_rows)
    return (covariance_field, adjoint_field)


def solution(mesh):
    placed = (P("tm", "row", None), P("row", None), P(), P(), P(), P(None, "row", None))
    return jax.shard_map(
        per_device,
        mesh=mesh,
        in_specs=placed,
        out_specs=(P("tm", "row", None), P("tm", "row", None)),
        check_vma=False,
    )
```

profile of v0, /device:TPU:8, one launch (start us, length us, event | category | flops | bytes accessed | tf_op | source)
XLA Modules:
  0.0 432.8 jit_solution(6217265600858629313)
XLA Ops:
  9.8 89.0 %all-gather.8.cloned.1.call-done = f32[2,512,512]{2,1,0:T(8,128)} async-done(((f32[2,8,512]{2,1,0:T(8,128)}), f32[2,512,512]{2,1,0:T(8,128)}) %all-gather.8.cloned.1.call-update) | async-done | bytes 2097168 | tf_op jit(solution)/shard_map/all_gather | solution.py:128
  98.9 2.0 convolution_bitcast_fusion.3
  100.9 2.0 fusion.2
  103.7 9.3 %reduce = f32[2048,32]{1,0:T(8,128)S(1)} reduce(f32[2048,1,32]{2,1,0:T(1,128)S(1)} %bitcast.153, f32[]{:T(128)} %broadcast.129), dimensions={1}, to_apply=%bitcast.132.reduce_sub_computation | reduce | bytes 524292
  113.4 21.7 %all_to_all.60 = f32[64,1,1024]{2,1,0:T(1,128)S(1)} all-to-all(f32[64,1,1024]{2,1,0:T(1,128)S(1)} %reshape.96), channel_id=1, replica_groups=mesh['tm'=8,'row'=64] {'row'}, dimensions={0} | all-to-all | bytes 524288 | tf_op jit(solution)/shard_map/all_to_all | solution.py:134
  136.3 1.8 reshape.97
  138.1 1.7 copy.114
  139.9 2.4 copy.82
  143.4 1.5 fusion.4
  146.2 10.2 %reduce.2 = f32[2048,32]{1,0:T(8,128)} reduce(f32[2048,1,32]{2,1,0:T(1,128)S(1)} %bitcast.154, f32[]{:T(128)} %broadcast.129), dimensions={1}, to_apply=%bitcast.134.reduce_sub_computation | reduce | bytes 524292
  156.4 2.4 reshape.98
  158.8 5.8 %all-to-all-start.1 = ((f32[64,1,1024]{2,1,0:T(1,128)}), f32[64,1,1024]{2,1,0:T(1,128)S(1)}, u32[]{:S(2)}, u32[]{:S(2)}) async-start(f32[64,1,1024]{2,1,0:T(1,128)} %reshape.98), calls=%async_computation.1 | async-start | bytes 524288 | tf_op jit(solution)/shard_map/all_to_all | solution.py:81
  165.6 11.4 %all-to-all-done.1 = f32[64,1,1024]{2,1,0:T(1,128)S(1)} async-done(((f32[64,1,1024]{2,1,0:T(1,128)}), f32[64,1,1024]{2,1,0:T(1,128)S(1)}, u32[]{:S(2)}, u32[]{:S(2)}) %all-to-all-start.1) | async-done | bytes 262176 | tf_op jit(solution)/shard_map/all_to_all | solution.py:81
  178.2 1.8 reshape.99
  180.0 1.7 copy.116
  181.7 2.2 copy.89
  184.5 12.1 %multiply_add_fusion.2 = (f32[2048,32]{0,1:T(8,128)}, f32[2048,32]{0,1:T(8,128)}) fusion(f32[2048,32]{0,1:T(8,128)S(1)} %squeeze.105, f32[]{:T(128)} %bitcast.20, s32[32,2048]{1,0:T(8,128)} %param.11, f32[]{:T(128)} %bitcast.19, f32[]{:T(128)} %bitcast.18, f32[]{:T(128)} %bitcast.17, f32[]{:T(128)} %bitcast.16, f32[]{:T(128)} %bitcast.15, f32[]{:T(128)} %bitcast.14, ...), kind=kLoop, calls=%fused_computation.28 | loop fusion | flops 2424832 | bytes 1048640 | tf_op jit(solution)/shard_map/add | solution.py:109
  197.4 22.9 %all-gather.12.cloned.1.call-done = f32[16384,32]{0,1:T(8,128)} async-done(((f32[2048,32]{0,1:T(8,128)}), f32[16384,32]{0,1:T(8,128)}) %all-gather.12.cloned.1.call-update) | async-done | bytes 2097168 | tf_op jit(solution)/shard_map/all_gather | solution.py:11
  220.3 6.2 %copy.117 = f32[16384,32]{1,0:T(8,128)} copy(f32[16384,32]{0,1:T(8,128)} %all-gather.12.cloned.1.call-done) | data formatting | bytes 4194304 | tf_op jit(solution)/shard_map/while | solution.py:20
  226.5 27.4 %all-gather.10.cloned.1.call-done = f32[16384,32]{0,1:T(8,128)} async-done(((f32[2048,32]{0,1:T(8,128)}), f32[16384,32]{0,1:T(8,128)}) %all-gather.10.cloned.1.call-update) | async-done | bytes 2097168 | tf_op jit(solution)/shard_map/all_gather | solution.py:11
  253.9 6.2 %copy.124 = f32[16384,32]{1,0:T(8,128)} copy(f32[16384,32]{0,1:T(8,128)} %all-gather.10.cloned.1.call-done) | data formatting | bytes 4194304 | tf_op jit(solution)/shard_map/while | solution.py:20
  261.3 2.0 multiply_add_fusion
  263.3 45.4 %all-gather.14.cloned.1.call-done = f32[16384,32]{0,1:T(8,128)} async-done(((f32[2048,32]{0,1:T(8,128)}), f32[16384,32]{0,1:T(8,128)}) %all-gather.14.cloned.1.call-update) | async-done | bytes 2097168 | tf_op jit(solution)/shard_map/all_gather | solution.py:11
  308.6 6.2 %copy.118 = f32[16384,32]{1,0:T(8,128)} copy(f32[16384,32]{0,1:T(8,128)} %all-gather.14.cloned.1.call-done) | data formatting | bytes 4194304 | tf_op jit(solution)/shard_map/while | solution.py:20
  314.9 14.7 %while.27 = (s32[]{:T(128)}, f32[2048,32]{1,0:T(8,128)S(1)}, s32[]{:T(128)}, f32[8,2048,32]{2,1,0:T(8,128)}, f32[8,2048,32]{2,1,0:T(8,128)}, /*index=5*/s32[]{:T(128)}, s32[]{:T(128)}, s32[]{:T(128)}, s32[]{:T(128)}) while((s32[]{:T(128)}, f32[2048,32]{1,0:T(8,128)S(1)}, s32[]{:T(128)}, f32[8,2048,32]{2,1,0:T(8,128)}, ...), condition=%wide.region_3.4_spmd, body=%wide.region_2.3_spmd.sunk | while | flops 131078 | bytes 1048719 | solution.py:20
  314.9 2.1 bitcast_add_fusion.5
  317.1 2.1 bitcast_add_fusion.5
  319.2 2.1 bitcast_add_fusion.5
  321.3 2.1 bitcast_add_fusion.5
  323.4 2.1 bitcast_add_fusion.5
  325.5 2.1 bitcast_add_fusion.5
  327.6 2.1 bitcast_add_fusion.5
  330.7 1.8 add_bitcast_fusion
  332.4 2.1 copy.98
  334.5 10.2 %reduce.4 = f32[2048,32]{1,0:T(8,128)} reduce(f32[2048,1,32]{2,1,0:T(1,128)S(1)} %bitcast.155, f32[]{:T(128)} %broadcast.129), dimensions={1}, to_apply=%bitcast.136.reduce_sub_computation | reduce | bytes 524292
  344.8 1.7 reshape.100
  346.5 25.9 %all_to_all.61 = f32[64,1,1024]{2,1,0:T(1,128)S(1)} all-to-all(f32[64,1,1024]{2,1,0:T(1,128)S(1)} %reshape.100), channel_id=1, replica_groups=mesh['tm'=8,'row'=64] {'row'}, dimensions={0} | all-to-all | bytes 524288 | tf_op jit(solution)/shard_map/all_to_all | solution.py:146
  373.6 1.8 reshape.101
  375.4 1.7 copy.119
  377.1 2.2 copy.100
  380.9 1.9 fusion.3
  384.1 10.2 %reduce.6 = f32[2048,32]{1,0:T(8,128)} reduce(f32[2048,1,32]{2,1,0:T(1,128)S(1)} %bitcast.156, f32[]{:T(128)} %broadcast.129), dimensions={1}, to_apply=%bitcast.138.reduce_sub_computation | reduce | bytes 524292
  394.3 1.7 reshape.102
  396.0 17.6 %all_to_all.62 = f32[64,1,1024]{2,1,0:T(1,128)S(1)} all-to-all(f32[64,1,1024]{2,1,0:T(1,128)S(1)} %reshape.102), channel_id=1, replica_groups=mesh['tm'=8,'row'=64] {'row'}, dimensions={0} | all-to-all | bytes 524288 | tf_op jit(solution)/shard_map/all_to_all | solution.py:81
  414.8 1.8 reshape.103
  416.6 1.7 copy.121
  418.3 2.2 copy.107
  423.3 2.1 fusion.8
  (44 shorter events, 21.7 us)
Async XLA Ops:
  7.2 93.7 %copy-start.3 = (f32[1,32,2048]{2,1,0:T(8,128)S(1)}, f32[1,32,2048]{2,1,0:T(8,128)}, u32[]{:S(2)}) copy-start(f32[1,32,2048]{2,1,0:T(8,128)} %param.10) | copy-start | bytes 786436
  7.2 91.7 %all-gather.8.cloned.1.call-start = ((), (), s32[]{:S(2)}) async-start(), calls=%async_computation.4 | async-start | bytes 2129920 | tf_op jit(solution)/shard_map/all_gather | solution.py:128
  139.9 2.8 copy-start
  146.2 18.7 %copy-start.4 = (f32[16]{0:T(128)S(1)}, f32[16]{0:T(128)}, u32[]{:S(2)}) copy-start(f32[16]{0:T(128)} %param.12) | copy-start | bytes 196
  158.8 18.2 %all-to-all-start.1 = ((f32[64,1,1024]{2,1,0:T(1,128)}), f32[64,1,1024]{2,1,0:T(1,128)S(1)}, u32[]{:S(2)}, u32[]{:S(2)}) async-start(f32[64,1,1024]{2,1,0:T(1,128)} %reshape.98), calls=%async_computation.1 | async-start | bytes 524288 | tf_op jit(solution)/shard_map/all_to_all | solution.py:81
  164.6 55.7 %all-gather.12.cloned.1.call-start = ((), (), s32[]{:S(2)}) async-start(), calls=%async_computation.6 | async-start | bytes 2359296 | tf_op jit(solution)/shard_map/all_gather | solution.py:11
  184.4 42.1 %copy-start.2 = (f32[2048,32]{0,1:T(8,128)}, f32[2048,32]{0,1:T(8,128)S(1)}, u32[]{:S(2)}) copy-start(f32[2048,32]{0,1:T(8,128)S(1)} %squeeze.105) | copy-start | bytes 786436
  196.6 57.3 %all-gather.10.cloned.1.call-start = ((), (), s32[]{:S(2)}) async-start(), calls=%async_computation.5 | async-start | bytes 2359296 | tf_op jit(solution)/shard_map/all_gather | solution.py:11
  197.3 111.3 %all-gather.14.cloned.1.call-start = ((), (), s32[]{:S(2)}) async-start(), calls=%async_computation.7 | async-start | bytes 2359296 | tf_op jit(solution)/shard_map/all_gather | solution.py:11
  260.2 1.0 copy-start.1
Sparse Core Ops, SparseCore 0:
  11.1 87.7 all-gather.7
  196.7 23.5 all-gather.11
  223.0 30.8 all-gather.9
  263.4 45.2 all-gather.13
where the time goes:
time: 440 us; the launch traced here: 433 us
  waiting for transfers between devices  198 us (45%)
  other arithmetic  75.8 us (17%)
  blocking collectives  65.3 us (15%)
  local copies, waits for them, and re-layouts  61.1 us (14%)
  between operations  14.3 us (3%)
  matrix products  12.6 us (3%)
  starting transfers between devices  6.13 us (1%)
    all_gather x3, waiting for transfers between devices, carried_in(): gathered = jax.tree.map(lambda a: lax.all_gather(a, axis), part)  95.7 us
    all_gather x1, waiting for transfers between devices, per_device(): offsets = lax.all_gather(inverse_offsets, 'row', axis=1, tiled=True)  89 us
    unnamed x4, other arithmetic  40 us
    all_to_all x1, blocking collectives, per_device(): lax.all_to_all(backward, 'row', split_axis=1, concat_axis=2, tiled=True)  25.9 us
    all_to_all x1, blocking collectives, per_device(): lax.all_to_all(row_solved, 'row', split_axis=1, concat_axis=2, tiled=True)  21.7 us
    while x5, local copies, waits for them, and re-layouts, carried_in(): return lax.fori_loop(0, ahead, one, state)  20.7 us
    all_to_all x1, blocking collectives, to_rows(): lax.all_to_all(column_field, 'row', split_axis=2, concat_axis=1, tiled=True)  17.6 us
    add x7, other arithmetic, affine_join(): return (earlier[0] * latter[0], latter[0] * earlier[1] + latter[1])  14.6 us
  transfers between devices with their start and end apart: 5, of which 5 were waited for; matrix products, arithmetic and copies ran while one was open for 2% of the time, Pallas kernels for 0%

commit v1 on v0

--- a/solution.py
+++ b/solution.py
@@ -125,7 +125,9 @@
 
 def per_device(forcing, rate_class, rate_table, row_class, col_class, inverse_offsets):
     row_count = forcing.shape[1]
-    offsets = lax.all_gather(inverse_offsets, "row", axis=1, tiled=True)
+    offsets = jnp.concatenate(
+        lax.all_to_all(jnp.stack([inverse_offsets] * lax.axis_size("row")), "row", 0, 0), axis=1
+    )
     first_row = lax.axis_index("row") * row_count
     my_rows = lax.dynamic_slice_in_dim(row_class, first_row, row_count)
     my_cols = lax.dynamic_slice_in_dim(col_class, first_row, row_count)

time: 440 us -> 423 us (0.961)
  waiting for transfers between devices: 198 us -> 158 us
  starting transfers between devices: 6.13 us -> 23 us
    all_gather x1 -> x0, waiting for transfers between devices: 89 us -> none  [per_device(): offsets = lax.all_gather(inverse_offsets, 'row', axis=1, tiled=True)]
    all_to_all x0 -> x1, waiting for transfers between devices: none -> 50.4 us  [per_device(): lax.all_to_all(jnp.stack([inverse_offsets] * lax.axis_size('row')), 'row'...]
    all_to_all x0 -> x1, starting transfers between devices: none -> 16.7 us  [per_device(): lax.all_to_all(jnp.stack([inverse_offsets] * lax.axis_size('row')), 'row'...]
    unnamed x19 -> x17, local copies, waits for them, and re-layouts: 13.9 us -> 15.2 us
where the time goes in v1:
time: 423 us; the launch traced here: 415 us
  waiting for transfers between devices  158 us (37%)
  other arithmetic  77.4 us (18%)
  blocking collectives  68.1 us (16%)
  local copies, waits for them, and re-layouts  63.7 us (15%)
  starting transfers between devices  23 us (5%)
  between operations  14.2 us (3%)
  matrix products  10.1 us (2%)
    all_gather x3, waiting for transfers between devices, carried_in(): gathered = jax.tree.map(lambda a: lax.all_gather(a, axis), part)  95.9 us
    all_to_all x1, waiting for transfers between devices, per_device(): lax.all_to_all(jnp.stack([inverse_offsets] * lax.axis_size('row')), 'row'...  50.4 us
    unnamed x4, other arithmetic  41.3 us
    all_to_all x1, blocking collectives, per_device(): lax.all_to_all(backward, 'row', split_axis=1, concat_axis=2, tiled=True)  25.9 us
    all_to_all x1, blocking collectives, per_device(): lax.all_to_all(row_solved, 'row', split_axis=1, concat_axis=2, tiled=True)  24.5 us
    while x5, local copies, waits for them, and re-layouts, carried_in(): return lax.fori_loop(0, ahead, one, state)  20.7 us
    all_to_all x1, blocking collectives, to_rows(): lax.all_to_all(column_field, 'row', split_axis=2, concat_axis=1, tiled=True)  17.6 us
    all_to_all x1, starting transfers between devices, per_device(): lax.all_to_all(jnp.stack([inverse_offsets] * lax.axis_size('row')), 'row'...  16.7 us
  transfers between devices with their start and end apart: 5, of which 5 were waited for; matrix products, arithmetic and copies ran while one was open for 2% of the time, Pallas kernels for 0%

profile of v1, /device:TPU:8, one launch (start us, length us, event | category | flops | bytes accessed | tf_op | source)
XLA Modules:
  0.0 415.0 jit_solution(3939373432856767647)
XLA Ops:
  7.2 2.4 stack.6
  9.5 16.7 %all-to-all-start = ((f32[64,2,8,512]{3,2,1,0:T(8,128)}), f32[64,2,8,512]{3,2,1,0:T(8,128)S(1)}, u32[]{:S(2)}, u32[]{:S(2)}) async-start(f32[64,2,8,512]{3,2,1,0:T(8,128)} %stack.6), calls=%async_computation | async-start | bytes 4194304 | tf_op jit(solution)/shard_map/all_to_all | solution.py:129
  27.2 50.4 %all-to-all-done = f32[64,2,8,512]{3,2,1,0:T(8,128)S(1)} async-done(((f32[64,2,8,512]{3,2,1,0:T(8,128)}), f32[64,2,8,512]{3,2,1,0:T(8,128)S(1)}, u32[]{:S(2)}, u32[]{:S(2)}) %all-to-all-start) | async-done | bytes 2097184 | tf_op jit(solution)/shard_map/all_to_all | solution.py:129
  80.1 10.3 %reduce = f32[2048,32]{1,0:T(8,128)} reduce(f32[2048,1,32]{2,1,0:T(1,128)S(1)} %bitcast.164, f32[]{:T(128)} %broadcast.131), dimensions={1}, to_apply=%bitcast.135.reduce_sub_computation | reduce | bytes 524292
  90.4 1.7 reshape.107
  92.1 24.5 %all_to_all.65 = f32[64,1,1024]{2,1,0:T(1,128)S(1)} all-to-all(f32[64,1,1024]{2,1,0:T(1,128)S(1)} %reshape.107), channel_id=1, replica_groups=mesh['tm'=8,'row'=64] {'row'}, dimensions={0} | all-to-all | bytes 524288 | tf_op jit(solution)/shard_map/all_to_all | solution.py:136
  117.8 1.8 reshape.108
  119.6 1.7 copy.114
  121.3 2.2 copy.82
  127.5 10.3 %reduce.2 = f32[2048,32]{1,0:T(8,128)} reduce(f32[2048,1,32]{2,1,0:T(1,128)S(1)} %bitcast.165, f32[]{:T(128)} %broadcast.131), dimensions={1}, to_apply=%bitcast.137.reduce_sub_computation | reduce | bytes 524292
  137.8 2.4 reshape.109
  140.2 5.9 %all-to-all-start.2 = ((f32[64,1,1024]{2,1,0:T(1,128)}), f32[64,1,1024]{2,1,0:T(1,128)S(1)}, u32[]{:S(2)}, u32[]{:S(2)}) async-start(f32[64,1,1024]{2,1,0:T(1,128)} %reshape.109), calls=%async_computation.2 | async-start | bytes 524288 | tf_op jit(solution)/shard_map/all_to_all | solution.py:81
  147.2 11.4 %all-to-all-done.2 = f32[64,1,1024]{2,1,0:T(1,128)S(1)} async-done(((f32[64,1,1024]{2,1,0:T(1,128)}), f32[64,1,1024]{2,1,0:T(1,128)S(1)}, u32[]{:S(2)}, u32[]{:S(2)}) %all-to-all-start.2) | async-done | bytes 262176 | tf_op jit(solution)/shard_map/all_to_all | solution.py:81
  159.8 1.8 reshape.110
  161.6 1.7 copy.116
  163.3 2.2 copy.89
  166.1 12.1 %multiply_add_fusion.2 = (f32[2048,32]{0,1:T(8,128)}, f32[2048,32]{0,1:T(8,128)}) fusion(f32[2048,32]{0,1:T(8,128)S(1)} %squeeze.105, f32[]{:T(128)} %bitcast.20, s32[32,2048]{1,0:T(8,128)} %param.11, f32[]{:T(128)} %bitcast.19, f32[]{:T(128)} %bitcast.18, f32[]{:T(128)} %bitcast.17, f32[]{:T(128)} %bitcast.16, f32[]{:T(128)} %bitcast.15, f32[]{:T(128)} %bitcast.14, ...), kind=kLoop, calls=%fused_computation.28 | loop fusion | flops 2424832 | bytes 1048640 | tf_op jit(solution)/shard_map/add | solution.py:109
  179.0 23.2 %all-gather.9.cloned.1.call-done = f32[16384,32]{0,1:T(8,128)} async-done(((f32[2048,32]{0,1:T(8,128)}), f32[16384,32]{0,1:T(8,128)}) %all-gather.9.cloned.1.call-update) | async-done | bytes 2097168 | tf_op jit(solution)/shard_map/all_gather | solution.py:11
  202.1 6.2 %copy.117 = f32[16384,32]{1,0:T(8,128)} copy(f32[16384,32]{0,1:T(8,128)} %all-gather.9.cloned.1.call-done) | data formatting | bytes 4194304 | tf_op jit(solution)/shard_map/while | solution.py:20
  208.4 27.4 %all-gather.7.cloned.1.call-done = f32[16384,32]{0,1:T(8,128)} async-done(((f32[2048,32]{0,1:T(8,128)}), f32[16384,32]{0,1:T(8,128)}) %all-gather.7.cloned.1.call-update) | async-done | bytes 2097168 | tf_op jit(solution)/shard_map/all_gather | solution.py:11
  235.7 6.2 %copy.124 = f32[16384,32]{1,0:T(8,128)} copy(f32[16384,32]{0,1:T(8,128)} %all-gather.7.cloned.1.call-done) | data formatting | bytes 4194304 | tf_op jit(solution)/shard_map/while | solution.py:20
  243.1 2.0 multiply_add_fusion
  245.1 45.4 %all-gather.11.cloned.1.call-done = f32[16384,32]{0,1:T(8,128)} async-done(((f32[2048,32]{0,1:T(8,128)}), f32[16384,32]{0,1:T(8,128)}) %all-gather.11.cloned.1.call-update) | async-done | bytes 2097168 | tf_op jit(solution)/shard_map/all_gather | solution.py:11
  290.5 6.2 %copy.118 = f32[16384,32]{1,0:T(8,128)} copy(f32[16384,32]{0,1:T(8,128)} %all-gather.11.cloned.1.call-done) | data formatting | bytes 4194304 | tf_op jit(solution)/shard_map/while | solution.py:20
  296.7 14.7 %while.27 = (s32[]{:T(128)}, f32[2048,32]{1,0:T(8,128)S(1)}, s32[]{:T(128)}, f32[8,2048,32]{2,1,0:T(8,128)}, f32[8,2048,32]{2,1,0:T(8,128)}, /*index=5*/s32[]{:T(128)}, s32[]{:T(128)}, s32[]{:T(128)}, s32[]{:T(128)}) while((s32[]{:T(128)}, f32[2048,32]{1,0:T(8,128)S(1)}, s32[]{:T(128)}, f32[8,2048,32]{2,1,0:T(8,128)}, ...), condition=%wide.region_3.4_spmd, body=%wide.region_2.3_spmd.sunk | while | flops 131078 | bytes 1048719 | solution.py:20
  296.8 2.1 bitcast_add_fusion.5
  298.9 2.1 bitcast_add_fusion.5
  301.0 2.1 bitcast_add_fusion.5
  303.1 2.1 bitcast_add_fusion.5
  305.2 2.1 bitcast_add_fusion.5
  307.3 2.1 bitcast_add_fusion.5
  309.4 2.1 bitcast_add_fusion.5
  312.5 1.8 add_bitcast_fusion
  314.3 2.1 copy.98
  316.4 10.3 %reduce.4 = f32[2048,32]{1,0:T(8,128)} reduce(f32[2048,1,32]{2,1,0:T(1,128)S(1)} %bitcast.166, f32[]{:T(128)} %broadcast.131), dimensions={1}, to_apply=%bitcast.139.reduce_sub_computation | reduce | bytes 524292
  326.7 1.7 reshape.111
  328.4 25.9 %all_to_all.66 = f32[64,1,1024]{2,1,0:T(1,128)S(1)} all-to-all(f32[64,1,1024]{2,1,0:T(1,128)S(1)} %reshape.111), channel_id=1, replica_groups=mesh['tm'=8,'row'=64] {'row'}, dimensions={0} | all-to-all | bytes 524288 | tf_op jit(solution)/shard_map/all_to_all | solution.py:148
  355.5 1.8 reshape.112
  357.4 1.7 copy.119
  359.1 2.2 copy.100
  362.9 1.9 fusion.3
  366.1 10.3 %reduce.6 = f32[2048,32]{1,0:T(8,128)} reduce(f32[2048,1,32]{2,1,0:T(1,128)S(1)} %bitcast.167, f32[]{:T(128)} %broadcast.131), dimensions={1}, to_apply=%bitcast.141.reduce_sub_computation | reduce | bytes 524292
  376.4 1.7 reshape.113
  378.1 17.6 %all_to_all.67 = f32[64,1,1024]{2,1,0:T(1,128)S(1)} all-to-all(f32[64,1,1024]{2,1,0:T(1,128)S(1)} %reshape.113), channel_id=1, replica_groups=mesh['tm'=8,'row'=64] {'row'}, dimensions={0} | all-to-all | bytes 524288 | tf_op jit(solution)/shard_map/all_to_all | solution.py:81
  396.9 1.8 reshape.114
  398.7 1.7 copy.121
  400.5 2.2 copy.107
  405.4 2.1 fusion.8
  (42 shorter events, 23.0 us)
Async XLA Ops:
  9.5 16.7 %copy-start.2 = (f32[1,32,2048]{2,1,0:T(8,128)S(1)}, f32[1,32,2048]{2,1,0:T(8,128)}, u32[]{:S(2)}) copy-start(f32[1,32,2048]{2,1,0:T(8,128)} %param.10) | copy-start | bytes 786436
  9.5 68.1 %all-to-all-start = ((f32[64,2,8,512]{3,2,1,0:T(8,128)}), f32[64,2,8,512]{3,2,1,0:T(8,128)S(1)}, u32[]{:S(2)}, u32[]{:S(2)}) async-start(f32[64,2,8,512]{3,2,1,0:T(8,128)} %stack.6), calls=%async_computation | async-start | bytes 4194304 | tf_op jit(solution)/shard_map/all_to_all | solution.py:129
  127.5 18.9 %copy-start.3 = (f32[16]{0:T(128)S(1)}, f32[16]{0:T(128)}, u32[]{:S(2)}) copy-start(f32[16]{0:T(128)} %param.12) | copy-start | bytes 196
  140.2 18.3 %all-to-all-start.2 = ((f32[64,1,1024]{2,1,0:T(1,128)}), f32[64,1,1024]{2,1,0:T(1,128)S(1)}, u32[]{:S(2)}, u32[]{:S(2)}) async-start(f32[64,1,1024]{2,1,0:T(1,128)} %reshape.109), calls=%async_computation.2 | async-start | bytes 524288 | tf_op jit(solution)/shard_map/all_to_all | solution.py:81
  146.2 56.0 %all-gather.9.cloned.1.call-start = ((), (), s32[]{:S(2)}) async-start(), calls=%async_computation.6 | async-start | bytes 2359296 | tf_op jit(solution)/shard_map/all_gather | solution.py:11
  166.0 42.3 %copy-start.1 = (f32[2048,32]{0,1:T(8,128)}, f32[2048,32]{0,1:T(8,128)S(1)}, u32[]{:S(2)}) copy-start(f32[2048,32]{0,1:T(8,128)S(1)} %squeeze.105) | copy-start | bytes 786436
  178.2 57.5 %all-gather.7.cloned.1.call-start = ((), (), s32[]{:S(2)}) async-start(), calls=%async_computation.5 | async-start | bytes 2359296 | tf_op jit(solution)/shard_map/all_gather | solution.py:11
  178.9 111.5 %all-gather.11.cloned.1.call-start = ((), (), s32[]{:S(2)}) async-start(), calls=%async_computation.7 | async-start | bytes 2359296 | tf_op jit(solution)/shard_map/all_gather | solution.py:11
  242.0 1.0 copy-start
Sparse Core Ops, SparseCore 0:
  178.3 23.7 all-gather.8
  204.8 30.8 all-gather.6
  245.2 45.2 all-gather.10
